TPU v7x, 32 devices: a whole 2x2x4 slice. The times are simulated.
32 devices in a mesh: tm: 8 (over y, x, core), mp: 4 (over z).
Axes of the slice: x: 2, y: 2, z: 4, core: 2. Of those that a mesh axis runs over, the one named last changes fastest.
Arguments:
- states: bfloat16 [16, 384, 3072], P('tm', None, 'mp'), may hold values from -6 to 6
- key_cache: bfloat16 [64, 384, 3072], P('tm', None, 'mp'), may hold values from -6 to 6
- value_cache: bfloat16 [64, 384, 3072], P('tm', None, 'mp'), may hold values from -6 to 6
- frame_times: int32 [16], replicated, may hold values from 0 to 15, each once
- valid_counts: int32 [384], P('tm'), may hold values from 1 to 64, as said below
- qkv_weight: bfloat16 [3072, 3, 3072], P(None, None, 'mp'), may hold values from -0.109375 to 0.109375
- out_weight: bfloat16 [3072, 3072], P('mp'), may hold values from -0.5 to 0.5
- up_weight: bfloat16 [3072, 6144], P(None, 'mp'), may hold values from -0.109375 to 0.109375
- down_weight: bfloat16 [6144, 3072], P('mp'), may hold values from -0.078125 to 0.078125
Outputs:
- next_states: bfloat16 [16, 384, 3072], P('tm', None, 'mp')
Inputs may be any that keep to these rules, and one draw needn't show every extreme that they name: `frame_times`: every new frame has a different time index. `valid_counts`: some patch may attend to all 64 cached frames and some to one.
All inputs are finite; a program needn't handle non-finite values.
Results may differ from a plain program's by a relative error of at most 0.015.
Values may be sent and summed in bfloat16 or wider, within the bound.
A program may use at most 192 MiB of HBM per device.

v0:
```python
import math

import jax
import jax.numpy as jnp
from jax import lax
from jax.sharding import PartitionSpec as P

HD = 128


def unit_heads(tensor):
    widened = tensor.astype(jnp.float32)
    mean_square = jnp.mean(widened * widened, axis=-1, keepdims=True)
    return (widened * lax.rsqrt(mean_square + 1e-06)).astype(jnp.bfloat16)


def normed_product(token_rows, weight):
    full_rows = lax.all_gather(token_rows, "mp", axis=1, tiled=True)
    normed = unit_heads(full_rows)
    return jnp.dot(normed, weight, preferred_element_type=jnp.float32)


def attend(projected, cached_keys, cached_values, frame_times, valid_counts):
    frame_count, patch_count, _, width = projected.shape
    cache_len = cached_keys.shape[0]
    local_heads = width // HD
    queries = unit_heads(projected[:, :, 0].reshape(frame_count, patch_count, local_heads, HD))
    fresh_keys = unit_heads(projected[:, :, 1].reshape(frame_count, patch_count, local_heads, HD))
    fresh_values = projected[:, :, 2].reshape(frame_count, patch_count, local_heads, HD)
    unit_cache = unit_heads(cached_keys.reshape(cache_len, patch_count, local_heads, HD))
    value_heads = cached_values.reshape(cache_len, patch_count, local_heads, HD)
    scale = 1.0 / math.sqrt(HD)
    cached_scores = (
        jnp.einsum("fphe,cphe->phfc", queries, unit_cache, preferred_element_type=jnp.float32)
        * scale
    )
    fresh_scores = (
        jnp.einsum("fphe,gphe->phfg", queries, fresh_keys, preferred_element_type=jnp.float32)
        * scale
    )
    cached_ok = (
        jnp.arange(cache_len, dtype=jnp.int32)[None, :] >= (cache_len - valid_counts)[:, None]
    )
    fresh_ok = frame_times[None, :] <= frame_times[:, None]
    cached_exp = jnp.where(cached_ok[:, None, None, :], jnp.exp(cached_scores), 0.0)
    fresh_exp = jnp.where(fresh_ok[None, None], jnp.exp(fresh_scores), 0.0)
    denominator = jnp.sum(cached_exp, axis=-1, keepdims=True) + jnp.sum(
        fresh_exp, axis=-1, keepdims=True
    )
    cached_weights = (cached_exp / denominator).astype(jnp.bfloat16)
    fresh_weights = (fresh_exp / denominator).astype(jnp.bfloat16)
    mixed = jnp.einsum(
        "phfc,cphe->fphe", cached_weights, value_heads, preferred_element_type=jnp.float32
    )
    mixed = mixed + jnp.einsum(
        "phfg,gphe->fphe", fresh_weights, fresh_values, preferred_element_type=jnp.float32
    )
    return mixed.astype(jnp.bfloat16).reshape(frame_count, patch_count, width)


def dense_tail(token_rows, heads_rows, out_weight, up_weight, down_weight):
    attn_term = jnp.dot(heads_rows, out_weight, preferred_element_type=jnp.float32)
    attn_sum = lax.psum_scatter(
        attn_term.astype(jnp.bfloat16), "mp", scatter_dimension=1, tiled=True
    ).astype(jnp.float32)
    middle = (token_rows.astype(jnp.float32) + attn_sum).astype(jnp.bfloat16)
    hidden = jax.nn.gelu(normed_product(middle, up_weight)).astype(jnp.bfloat16)
    ffn_term = jnp.dot(hidden, down_weight, preferred_element_type=jnp.float32)
    ffn_sum = lax.psum_scatter(
        ffn_term.astype(jnp.bfloat16), "mp", scatter_dimension=1, tiled=True
    ).astype(jnp.float32)
    return (middle.astype(jnp.float32) + ffn_sum).astype(jnp.bfloat16)


def body(
    states,
    key_cache,
    value_cache,
    frame_times,
    valid_counts,
    qkv_weight,
    out_weight,
    up_weight,
    down_weight,
):
    width = states.shape[2]
    joined_weight = qkv_weight.reshape(qkv_weight.shape[0], 3 * width)
    cached_keys, cached_values = (
        lax.all_to_all(key_cache, "tm", split_axis=1, concat_axis=0, tiled=True),
        lax.all_to_all(value_cache, "tm", split_axis=1, concat_axis=0, tiled=True),
    )
    frame_rows = states.reshape(-1, width)
    projected = normed_product(frame_rows, joined_weight).astype(jnp.bfloat16)
    projected = projected.reshape(states.shape[0], states.shape[1], 3, width)
    owned_projected = lax.all_to_all(projected, "tm", split_axis=1, concat_axis=0, tiled=True)
    heads_out = attend(owned_projected, cached_keys, cached_values, frame_times, valid_counts)
    returned = lax.all_to_all(heads_out, "tm", split_axis=0, concat_axis=1, tiled=True)
    result = dense_tail(frame_rows, returned.reshape(-1, width), out_weight, up_weight, down_weight)
    return result.reshape(states.shape)


def solution(mesh):
    in_specs = (
        P("tm", None, "mp"),
        P("tm", None, "mp"),
        P("tm", None, "mp"),
        P(),
        P("tm"),
        P(None, None, "mp"),
        P("mp", None),
        P(None, "mp"),
        P("mp", None),
    )
    out_specs = P("tm", None, "mp")
    return jax.shard_map(body, mesh=mesh, in_specs=in_specs, out_specs=out_specs, check_vma=False)
```

profile of v0, /device:TPU:0, one launch (start us, length us, event | category | flops | bytes accessed | tf_op | source)
XLA Modules:
  0.0 574.9 jit_solution(12445548082595304249)
XLA Ops:
  7.3 7.1 %copy.104 = bf16[8,384,768]{2,0,1:T(8,128)(2,1)} copy(bf16[8,384,768]{2,1,0:T(8,128)(2,1)} %param.10) | data formatting | bytes 9437184 | tf_op args[1]
  14.4 5.2 all-to-all-start.1
  19.5 18.7 %copy.97 = bf16[3072,3,768]{0,2,1:T(8,128)(2,1)} copy(bf16[3072,3,768]{2,0,1:T(8,128)(2,1)} %param.14) | data formatting | bytes 28311552 | tf_op args[5]
  38.2 7.1 %copy.114 = bf16[8,384,768]{2,0,1:T(8,128)(2,1)} copy(bf16[8,384,768]{2,1,0:T(8,128)(2,1)} %param.11) | data formatting | bytes 9437184 | tf_op args[2]
  45.3 29.1 %all-to-all-done.1 = bf16[8,384,768]{2,0,1:T(8,128)(2,1)} async-done(((bf16[8,384,768]{2,0,1:T(8,128)(2,1)}), bf16[8,384,768]{2,0,1:T(8,128)(2,1)}, u32[]{:S(2)}, u32[]{:S(2)}) %all-to-all-start.1) | async-done | bytes 4718624 | tf_op jit(solution)/shard_map/all_to_all | solution.py:89
  74.4 4.8 all-to-all-start.2
  79.2 21.8 %all-gather.3.cloned.1.call-done = bf16[768,3072]{1,0:T(8,128)(2,1)} async-done(((bf16[768,768]{1,0:T(8,128)(2,1)}), bf16[768,3072]{1,0:T(8,128)(2,1)}) %all-gather.3.cloned.1.call-update) | async-done | bytes 4718608 | tf_op jit(solution)/shard_map/all_gather | solution.py:18
  101.1 3.5 fusion
  104.8 14.3 %convolution_convert_fusion = bf16[768,2304]{1,0:T(8,128)(2,1)S(1)} fusion(bf16[3072,2304]{0,1:T(8,128)(2,1)} %bitcast.50, bf16[768,3072]{1,0:T(8,128)(2,1)S(1)} %copy-done.2, f32[768]{0:T(1024)S(1)} %add_rsqrt_fusion.4), kind=kOutput, calls=%fused_computation.12 | convolution fusion | flops 10880483328 | bytes 22416384 | tf_op jit(solution)/shard_map/dot_general | solution.py:20
  119.2 5.4 reshape.134
  124.6 9.5 %copy.99 = bf16[2,384,3,768]{3,0,2,1:T(2,128)(2,1)} copy(bf16[2,384,3,768]{3,2,1,0:T(4,128)(2,1)} %reshape.134) | data formatting | bytes 7077888 | tf_op jit(solution)/shard_map/reshape | solution.py:94
  134.1 3.8 all-to-all-start
  138.2 7.2 %copy.148 = f32[8,8,48,768]{3,2,0,1:T(8,128)} copy(bf16[8,8,48,768]{3,0,2,1:T(8,128)(2,1)} %bitcast.16) | data formatting | bytes 14155776 | tf_op jit(solution)/shard_map/convert_element_type | solution.py:12
  145.4 12.0 %reshape.131 = f32[64,48,6,128]{3,2,1,0:T(8,128)} reshape(f32[8,8,48,768]{3,2,1,0:T(8,128)} %bitcast.48) | data formatting | bytes 18874368 | tf_op jit(solution)/shard_map/convert_element_type | solution.py:12
  157.4 9.1 %multiply_reduce_fusion = f32[64,48,6]{2,1,0:T(8,128)} fusion(f32[64,48,6,128]{3,2,1,0:T(8,128)} %reshape.131), kind=kLoop, calls=%fused_computation.1 | loop fusion | flops 4700160 | bytes 9510912 | tf_op jit(solution)/shard_map/reduce_sum | solution.py:13
  173.5 5.6 copy.149
  179.0 10.8 %reshape.126 = bf16[64,48,6,128]{3,2,1,0:T(8,128)(2,1)} reshape(bf16[8,8,48,768]{3,2,1,0:T(8,128)(2,1)} %bitcast.49) | data formatting | bytes 9437184 | tf_op jit(solution)/shard_map/reshape | solution.py:31
  189.8 10.3 %multiply_convert_fusion = bf16[64,48,6,128]{3,2,1,0:T(8,128)(2,1)} fusion(f32[64,48,6,128]{3,2,1,0:T(8,128)} %reshape.131, f32[64,48,6]{2,1,0:T(8,128)} %copy.107), kind=kLoop, calls=%fused_computation | loop fusion | flops 4718592 | bytes 14229504 | tf_op jit(solution)/shard_map/convert_element_type | solution.py:14
  200.9 2.9 slice_convert_fusion.1
  210.4 3.8 reshape.132
  214.2 3.5 multiply_reduce_fusion.1
  222.7 3.8 reshape_squeeze.2
  226.5 4.2 multiply_convert_fusion.1
  232.7 7.1 %fusion.30 = (f32[48,6,16]{2,1,0:T(8,128)S(1)}, f32[48,6,16,64]{3,2,1,0:T(8,128)S(1)}) fusion(pred[48,64]{1,0:T(8,128)(4,1)S(1)} %iota_compare_fusion, bf16[64,48,6,128]{3,2,1,0:T(8,128)(2,1)} %multiply_convert_fusion, bf16[16,48,6,128]{3,2,1,0:T(8,128)(2,1)S(1)} %get-tuple-element.13), kind=kOutput, calls=%fused_computation.47 | convolution fusion | flops 76377600 | bytes 7099392 | tf_op jit(solution)/shard_map/fphe,cphe->phfc/dot_general | solution.py:34
  241.5 4.2 fusion.25
  247.5 20.7 %all_to_all.57 = bf16[16,48,768]{2,1,0:T(8,128)(2,1)S(1)} all-to-all(bf16[16,48,768]{2,1,0:T(8,128)(2,1)S(1)} %reshape.127), channel_id=1, replica_groups=mesh['tm'=8,'mp'=4] {'tm'}, dimensions={0} | all-to-all | bytes 2359296 | tf_op jit(solution)/shard_map/all_to_all | solution.py:97
  268.3 7.9 %convolution_convert_fusion.1 = bf16[768,3072]{1,0:T(8,128)(2,1)} fusion(bf16[768,768]{1,0:T(8,128)(2,1)S(1)} %bitcast.57, bf16[768,3072]{1,0:T(8,128)(2,1)} %param.15), kind=kOutput, calls=%fused_computation.13 | convolution fusion | flops 3626237952 | bytes 10616832 | tf_op jit(solution)/shard_map/dot_general | solution.py:62
  276.2 85.2 %reduce-scatter.3.cloned.1.call-done = bf16[768,768]{1,0:T(8,128)(2,1)} async-done(((bf16[768,3072]{1,0:T(8,128)(2,1)}), bf16[768,768]{1,0:T(8,128)(2,1)}) %reduce-scatter.3.cloned.1.call-update) | async-done | bytes 1179664 | tf_op jit(solution)/shard_map/reduce_scatter | solution.py:63
  364.0 90.0 %all-gather.5.cloned.1.call-done = bf16[768,3072]{1,0:T(8,128)(2,1)} async-done(((bf16[768,768]{1,0:T(8,128)(2,1)}), bf16[768,3072]{1,0:T(8,128)(2,1)}) %all-gather.5.cloned.1.call-update) | async-done | bytes 4718608 | tf_op jit(solution)/shard_map/all_gather | solution.py:18
  454.1 3.3 fusion.2
  457.4 24.4 %convolution_convert_fusion.2 = bf16[768,3072]{1,0:T(8,128)(2,1)} fusion(bf16[1536,3072]{1,0:T(8,128)(2,1)} %param.17, bf16[3072,1536]{1,0:T(8,128)(2,1)} %param.16, bf16[768,3072]{1,0:T(8,128)(2,1)} %all-gather.5.cloned.1.call-done, f32[768]{0:T(1024)S(1)} %add_rsqrt_fusion.3), kind=kOutput, calls=%fused_computation.14 | convolution fusion | flops 14515568640 | bytes 28314624 | tf_op jit(solution)/shard_map/dot_general | solution.py:68
  481.8 83.8 %reduce-scatter.5.cloned.1.call-done = bf16[768,768]{1,0:T(8,128)(2,1)} async-done(((bf16[768,3072]{1,0:T(8,128)(2,1)}), bf16[768,768]{1,0:T(8,128)(2,1)}) %reduce-scatter.5.cloned.1.call-update) | async-done | bytes 1179664 | tf_op jit(solution)/shard_map/reduce_scatter | solution.py:69
  (53 shorter events, 31.3 us)
Async XLA Ops:
  6.5 94.5 %all-gather.3.cloned.1.call-start = ((), (), s32[]{:S(2)}) async-start(), calls=%async_computation.6 | async-start | bytes 5898240 | tf_op jit(solution)/shard_map/all_gather | solution.py:18
  14.4 60.0 %all-to-all-start.1 = ((bf16[8,384,768]{2,0,1:T(8,128)(2,1)}), bf16[8,384,768]{2,0,1:T(8,128)(2,1)}, u32[]{:S(2)}, u32[]{:S(2)}) async-start(bf16[8,384,768]{2,0,1:T(8,128)(2,1)} %copy.104), calls=%async_computation.1 | async-start | bytes 9437184 | tf_op jit(solution)/shard_map/all_to_all | solution.py:89
  74.4 59.7 %all-to-all-start.2 = ((bf16[8,384,768]{2,0,1:T(8,128)(2,1)}), bf16[8,384,768]{2,0,1:T(8,128)(2,1)}, u32[]{:S(2)}, u32[]{:S(2)}) async-start(bf16[8,384,768]{2,0,1:T(8,128)(2,1)} %copy.114), calls=%async_computation.2 | async-start | bytes 9437184 | tf_op jit(solution)/shard_map/all_to_all | solution.py:90
  101.1 3.8 copy-start.2
  134.1 3.9 copy-start.5
  134.1 3.9 copy-start.4
  134.1 66.0 %all-to-all-start = ((bf16[2,384,3,768]{3,0,2,1:T(2,128)(2,1)}), bf16[2,384,3,768]{3,0,2,1:T(2,128)(2,1)S(1)}, u32[]{:S(2)}, u32[]{:S(2)}) async-start(bf16[2,384,3,768]{3,0,2,1:T(2,128)(2,1)} %copy.99), calls=%async_computation | async-start | bytes 7077888 | tf_op jit(solution)/shard_map/all_to_all | solution.py:95
  137.9 223.4 %reduce-scatter.3.cloned.1.call-start = ((), (), s32[]{:S(2)}) async-start(), calls=%async_computation.7 | async-start | bytes 5898240 | tf_op jit(solution)/shard_map/reduce_scatter | solution.py:63
  232.7 7.2 %copy-start.3 = (bf16[16,48,6,128]{3,2,1,0:T(8,128)(2,1)S(1)}, bf16[16,48,6,128]{3,2,1,0:T(8,128)(2,1)}, u32[]{:S(2)}) copy-start(bf16[16,48,6,128]{3,2,1,0:T(8,128)(2,1)} %reshape_squeeze.2) | copy-start | bytes 3538948
  232.7 8.4 %slice-start = ((s8[6291456]{0:T(1024)(128)(4,1)}), s8[4194304]{0:T(1024)(128)(4,1)S(1)}, s32[]{:S(2)}) async-start(s8[6291456]{0:T(1024)(128)(4,1)} %bitcast.53), calls=%async_computation.10 | async-start | bytes 8388608
  239.9 1.6 slice-start.1
  276.1 85.3 %copy-start.1 = (bf16[2,384,768]{2,1,0:T(8,128)(2,1)S(1)}, bf16[2,384,768]{2,1,0:T(8,128)(2,1)}, u32[]{:S(2)}) copy-start(bf16[2,384,768]{2,1,0:T(8,128)(2,1)} %param.9) | copy-start | bytes 3538948
  276.1 177.9 %all-gather.5.cloned.1.call-start = ((), (), s32[]{:S(2)}) async-start(), calls=%async_computation.8 | async-start | bytes 5898240 | tf_op jit(solution)/shard_map/all_gather | solution.py:18
  364.0 201.6 %reduce-scatter.5.cloned.1.call-start = ((), (), s32[]{:S(2)}) async-start(), calls=%async_computation.9 | async-start | bytes 5898240 | tf_op jit(solution)/shard_map/reduce_scatter | solution.py:69
  481.8 83.9 %copy-start = (bf16[768,768]{1,0:T(8,128)(2,1)S(1)}, bf16[768,768]{1,0:T(8,128)(2,1)}, u32[]{:S(2)}) copy-start(bf16[768,768]{1,0:T(8,128)(2,1)} %add_convert_fusion.1) | copy-start | bytes 3538948
Sparse Core Ops, SparseCore 0:
  8.9 92.0 all-gather.2
  276.3 85.0 reduce-scatter.2
  364.1 89.9 all-gather.4
  481.9 83.6 reduce-scatter.4
where the time goes:
time: 582 us; the launch traced here: 575 us
  waiting for transfers between devices  311 us (53%)
  local copies, waits for them, and re-layouts  107 us (18%)
  matrix products  61.1 us (10%)
  other arithmetic  47.5 us (8%)
  blocking collectives  20.7 us (4%)
  starting transfers between devices  13.9 us (2%)
  between operations  13.5 us (2%)
    all_gather x2, waiting for transfers between devices, normed_product(): full_rows = lax.all_gather(token_rows, 'mp', axis=1, tiled=True)  112 us
    reduce_scatter x1, waiting for transfers between devices, dense_tail(): lax.psum_scatter(attn_term.astype(jnp.bfloat16), 'mp', scatter_dimension=...  85.2 us
    reduce_scatter x1, waiting for transfers between devices, dense_tail(): lax.psum_scatter(ffn_term.astype(jnp.bfloat16), 'mp', scatter_dimension=1...  83.8 us
    unnamed x19, local copies, waits for them, and re-layouts  33.6 us
    all_to_all x1, waiting for transfers between devices, body(): lax.all_to_all(key_cache, 'tm', split_axis=1, concat_axis=0, tiled=True)  29.1 us
    convert_element_type x4, local copies, waits for them, and re-layouts, unit_heads(): widened = tensor.astype(jnp.float32)  25.5 us
    dot_general x1, matrix products, dense_tail(): ffn_term = jnp.dot(hidden, down_weight, preferred_element_type=jnp.float32)  24.4 us
    all_to_all x1, blocking collectives, body(): lax.all_to_all(heads_out, 'tm', split_axis=0, concat_axis=1, tiled=True)  20.7 us
  transfers between devices with their start and end apart: 7, of which 5 were waited for; matrix products, arithmetic and copies ran while one was open for 22% of the time, Pallas kernels for 0%

commit v1 on v0

v1 whole, which is shorter than its diff:
```python
import functools
import math

import jax
import jax.numpy as jnp
from jax import lax
from jax.experimental import pallas as pl
from jax.experimental.pallas import tpu as pltpu
from jax.sharding import PartitionSpec as P

HD = 128
MESH = pl.DeviceIdType.MESH
CHUNKS = 8


def unit_rows(tensor):
    widened = tensor.astype(jnp.float32)
    mean_square = jnp.mean(widened * widened, axis=-1, keepdims=True)
    return (widened * lax.rsqrt(mean_square + 1e-06)).astype(jnp.bfloat16)


def attend_kernel(patches, counts_ref, mask_ref, fresh_ref, keys_ref, values_ref, out_ref):
    devices, _, share, width = keys_ref.shape
    frames = fresh_ref.shape[1]
    cache = devices * share
    heads = width // HD
    scale = 1.0 / math.sqrt(HD)
    fresh_ok = mask_ref[...] > 0.5
    lane = lax.broadcasted_iota(jnp.int32, mask_ref.shape, 1)
    for p in range(patches):
        count = counts_ref[pl.program_id(0) * patches + p]
        allowed = ((lane >= cache - count) & (lane < cache)) | fresh_ok
        fresh = fresh_ref[p].astype(jnp.float32)
        old_keys = keys_ref[:, p].astype(jnp.float32).reshape(cache, width)
        old_values = values_ref[:, p].astype(jnp.float32).reshape(cache, width)
        all_keys = jnp.concatenate([old_keys, fresh[:, width : 2 * width]], axis=0)
        all_values = jnp.concatenate([old_values, fresh[:, 2 * width :]], axis=0).astype(jnp.bfloat16)
        scores = []
        for h in range(heads):
            at = slice(h * HD, (h + 1) * HD)
            scores.append(
                lax.dot_general(
                    unit_rows(fresh[:, at]),
                    unit_rows(all_keys[:, at]),
                    (((1,), (1,)), ((), ())),
                    preferred_element_type=jnp.float32,
                )
            )
        raised = jnp.where(allowed, jnp.exp(jnp.concatenate(scores, axis=0) * scale), 0.0)
        weights = (raised / jnp.sum(raised, axis=-1, keepdims=True)).astype(jnp.bfloat16)
        for h in range(heads):
            at = slice(h * HD, (h + 1) * HD)
            out_ref[p, :, at] = jnp.dot(
                weights[h * frames : (h + 1) * frames], all_values[:, at], preferred_element_type=jnp.float32
            ).astype(jnp.bfloat16)


def attend(fresh, cached_keys, cached_values, frame_times, valid_counts):
    patch_count, frames, _ = fresh.shape
    devices, _, share, width = cached_keys.shape
    cache = devices * share
    heads = width // HD
    patches = 4
    fresh_ok = (frame_times[None, :] <= frame_times[:, None]).astype(jnp.float32)
    mask = jnp.concatenate([jnp.zeros((frames, cache), jnp.float32), fresh_ok], axis=1)
    mask = jnp.tile(mask, (heads, 1))
    cache_spec = pl.BlockSpec((devices, patches, share, width), lambda s: (0, s, 0, 0))
    return pl.pallas_call(
        functools.partial(attend_kernel, patches),
        grid=(patch_count // patches,),
        in_specs=[
            pl.BlockSpec(memory_space=pltpu.SMEM),
            pl.BlockSpec(mask.shape, lambda s: (0, 0)),
            pl.BlockSpec((patches, frames, 3 * width), lambda s: (s, 0, 0)),
            cache_spec,
            cache_spec,
        ],
        out_specs=pl.BlockSpec((patches, frames, width), lambda s: (s, 0, 0)),
        out_shape=jax.ShapeDtypeStruct((patch_count, frames, width), jnp.bfloat16),
        compiler_params=pltpu.CompilerParams(vmem_limit_bytes=40 * 2**20),
        name="attend",
    )(valid_counts, mask, fresh, cached_keys, cached_values)


def tail_kernel(
    n, chunks,
    heads_ref, states_ref, out_w_hbm, up_w_hbm, down_w_hbm, result_ref,
    out_w, up_w, down_w, terms, landed, middle,
    weight_sem, sum_send, sum_recv, right_send, left_send, gather_recv,
):
    me = lax.axis_index("mp")
    rows, width = states_ref.shape[1:]
    last = n - 1

    loads = [
        pltpu.make_async_copy(src, dst, weight_sem.at[k])
        for k, (src, dst) in enumerate(((out_w_hbm, out_w), (up_w_hbm, up_w), (down_w_hbm, down_w)))
    ]
    for load in loads:
        load.start()

    barrier = pltpu.get_barrier_semaphore()

    @pl.when(me > 0)
    def _():
        pl.semaphore_signal(barrier, inc=1, device_id={"mp": me - 1}, device_id_type=MESH)

    @pl.when(me < last)
    def _():
        pl.semaphore_signal(barrier, inc=1, device_id={"mp": me + 1}, device_id_type=MESH)

    @pl.when((me > 0) & (me < last))
    def _():
        pl.semaphore_wait(barrier, 2)

    @pl.when((me == 0) | (me == last))
    def _():
        pl.semaphore_wait(barrier, 1)

    def sum_copy(c, d, slot, target):
        return pltpu.make_async_remote_copy(
            src_ref=terms.at[c, d],
            dst_ref=landed.at[c, slot],
            send_sem=sum_send.at[c, d],
            recv_sem=sum_recv.at[c, slot],
            device_id={"mp": target},
            device_id_type=MESH,
        )

    def gather_copy(c, d, send_sem, target):
        return pltpu.make_async_remote_copy(
            src_ref=middle.at[c, d],
            dst_ref=middle.at[c, d],
            send_sem=send_sem.at[c, d],
            recv_sem=gather_recv.at[c, d],
            device_id={"mp": target},
            device_id_type=MESH,
        )

    def active(c):
        return (c >= 0) & (c < chunks)

    def add_landed(c, d, slot):
        sum_copy(c, d, slot, me).wait_recv()
        terms[c, d] = (
            terms[c, d].astype(jnp.float32) + landed[c, slot].astype(jnp.float32)
        ).astype(jnp.bfloat16)

    def sum_right(tick):
        c = tick - me
        for d in range(last, 0, -1):
            @pl.when(active(c) & (me < d))
            def _():
                @pl.when(me > 0)
                def _():
                    add_landed(c, d, d)

                sum_copy(c, d, d, me + 1).start()

    def sum_left(tick):
        c = tick - (last - me)
        for d in range(last):
            @pl.when(active(c) & (me > d))
            def _():
                @pl.when(me < last)
                def _():
                    add_landed(c, d, d)

                @pl.when(me - 1 == d)
                def _():
                    sum_copy(c, d, n, me - 1).start()

                @pl.when(me - 1 > d)
                def _():
                    sum_copy(c, d, d, me - 1).start()

    def sum_end(c):
        @pl.when(me > 0)
        def _():
            sum_copy(c, me, me, me).wait_recv()

        @pl.when(me < last)
        def _():
            sum_copy(c, me, n, me).wait_recv()

        zero = jnp.zeros((rows, width), jnp.float32)
        from_left = jnp.where(me > 0, landed[c, me].astype(jnp.float32), zero)
        from_right = jnp.where(me < last, landed[c, n].astype(jnp.float32), zero)
        return terms[c, me].astype(jnp.float32) + from_left + from_right

    def wait_sum_sends(c):
        for d in range(n):
            @pl.when(me != d)
            def _():
                sum_copy(c, d, d, me).wait_send()

    def step(tick, carry):
        base = tick - 2 * last


        for h in range(last, 0, -1):
            c = tick - last - h

            @pl.when(active(c) & (me - h >= 0))
            def _():
                gather_copy(c, me - h, right_send, me).wait_recv()

                @pl.when(me < last)
                def _():
                    gather_copy(c, me - h, right_send, me + 1).start()

            @pl.when(active(c) & (me + h <= last))
            def _():
                gather_copy(c, me + h, left_send, me).wait_recv()

                @pl.when(me > 0)
                def _():
                    gather_copy(c, me + h, left_send, me - 1).start()

        @pl.when(tick < chunks)
        def _():
            block = heads_ref[tick]
            for d in range(n):
                terms[tick, d] = jnp.dot(
                    block, out_w[:, d * width : (d + 1) * width], preferred_element_type=jnp.float32
                ).astype(jnp.bfloat16)

        sum_right(tick)
        sum_left(tick)

        c_mid = tick - last

        @pl.when(active(c_mid))
        def _():
            total = sum_end(c_mid)
            middle[c_mid, me] = (states_ref[c_mid].astype(jnp.float32) + total).astype(jnp.bfloat16)

            @pl.when(me < last)
            def _():
                gather_copy(c_mid, me, right_send, me + 1).start()

            @pl.when(me > 0)
            def _():
                gather_copy(c_mid, me, left_send, me - 1).start()

        @pl.when(active(base))
        def _():
            wait_sum_sends(base)
            squares = jnp.zeros((rows, 1), jnp.float32)
            for d in range(n):
                block = middle[base, d].astype(jnp.float32)
                squares = squares + jnp.sum(block * block, axis=-1, keepdims=True)
            factor = lax.rsqrt(squares / (n * width) + 1e-06)
            hidden = None
            for d in range(n):
                normed = (middle[base, d].astype(jnp.float32) * factor).astype(jnp.bfloat16)
                part = jnp.dot(
                    normed, up_w[d * width : (d + 1) * width, :], preferred_element_type=jnp.float32
                )
                hidden = part if hidden is None else hidden + part
            hidden = jax.nn.gelu(hidden).astype(jnp.bfloat16)
            for d in range(n):
                terms[base, d] = jnp.dot(
                    hidden, down_w[:, d * width : (d + 1) * width], preferred_element_type=jnp.float32
                ).astype(jnp.bfloat16)

        sum_right(base)
        sum_left(base)

        c_end = base - last

        @pl.when(active(c_end))
        def _():
            total = sum_end(c_end)
            result_ref[c_end] = (middle[c_end, me].astype(jnp.float32) + total).astype(jnp.bfloat16)

        return carry

    loads[0].wait()
    lax.fori_loop(0, 2 * last, step, 0)
    loads[1].wait()
    loads[2].wait()
    lax.fori_loop(2 * last, chunks + 3 * last, step, 0)

    def drain(c, carry):
        wait_sum_sends(c)
        for d in range(n):
            @pl.when((d <= me) & (me < last))
            def _():
                gather_copy(c, d, right_send, me).wait_send()

            @pl.when((d >= me) & (me > 0))
            def _():
                gather_copy(c, d, left_send, me).wait_send()
        return carry

    lax.fori_loop(0, chunks, drain, 0)


def tail(n, states, heads_rows, out_weight, up_weight, down_weight):
    count, width = states.shape
    rows = count // CHUNKS
    states = states.reshape(CHUNKS, rows, width)
    heads_rows = heads_rows.reshape(CHUNKS, rows, width)
    vmem = pl.BlockSpec(memory_space=pltpu.VMEM)
    hbm = pl.BlockSpec(memory_space=pl.ANY)
    result = pl.pallas_call(
        functools.partial(tail_kernel, n, CHUNKS),
        out_shape=jax.ShapeDtypeStruct(states.shape, jnp.bfloat16),
        in_specs=[vmem, vmem, hbm, hbm, hbm],
        out_specs=vmem,
        scratch_shapes=[
            pltpu.VMEM(out_weight.shape, jnp.bfloat16),
            pltpu.VMEM(up_weight.shape, jnp.bfloat16),
            pltpu.VMEM(down_weight.shape, jnp.bfloat16),
            pltpu.VMEM((CHUNKS, n, rows, width), jnp.bfloat16),
            pltpu.VMEM((CHUNKS, n + 1, rows, width), jnp.bfloat16),
            pltpu.VMEM((CHUNKS, n, rows, width), jnp.bfloat16),
            pltpu.SemaphoreType.DMA((3,)),
            pltpu.SemaphoreType.DMA((CHUNKS, n)),
            pltpu.SemaphoreType.DMA((CHUNKS, n + 1)),
            pltpu.SemaphoreType.DMA((CHUNKS, n)),
            pltpu.SemaphoreType.DMA((CHUNKS, n)),
            pltpu.SemaphoreType.DMA((CHUNKS, n)),
        ],
        compiler_params=pltpu.CompilerParams(
            collective_id=1, has_side_effects=True, vmem_limit_bytes=60 * 2**20
        ),
        name="tail",
    )(heads_rows, states, out_weight, up_weight, down_weight)
    return result.reshape(count, width)


def to_patches(cache, devices):
    frames, patch_count, width = cache.shape
    blocks = cache.reshape(frames, devices, patch_count // devices, width).transpose(1, 2, 0, 3)
    return lax.all_to_all(blocks, "tm", split_axis=0, concat_axis=0)


def body(
    n, devices,
    states, key_cache, value_cache, frame_times, valid_counts,
    qkv_weight, out_weight, up_weight, down_weight,
):
    frames, patch_count, width = states.shape
    share = patch_count // devices
    joined_weight = qkv_weight.reshape(qkv_weight.shape[0], 3 * width)
    frame_rows = states.reshape(-1, width)
    full_rows = lax.all_gather(frame_rows, "mp", axis=1, tiled=True)
    cached_keys = to_patches(key_cache, devices)
    cached_values = to_patches(value_cache, devices)
    projected = jnp.dot(unit_rows(full_rows), joined_weight, preferred_element_type=jnp.float32)
    projected = projected.astype(jnp.bfloat16).reshape(frames, devices, share, 3 * width)
    owned = lax.all_to_all(projected.transpose(1, 0, 2, 3), "tm", split_axis=0, concat_axis=0)
    fresh = owned.reshape(devices * frames, share, 3 * width).transpose(1, 0, 2)
    heads_out = attend(fresh, cached_keys, cached_values, frame_times, valid_counts)
    heads_out = heads_out.transpose(1, 0, 2).reshape(devices, frames, share, width)
    returned = lax.all_to_all(heads_out, "tm", split_axis=0, concat_axis=0)
    heads_rows = returned.transpose(1, 0, 2, 3).reshape(-1, width)
    result = tail(n, frame_rows, heads_rows, out_weight, up_weight, down_weight)
    return result.reshape(states.shape)


def solution(mesh):
    in_specs = (
        P("tm", None, "mp"),
        P("tm", None, "mp"),
        P("tm", None, "mp"),
        P(),
        P("tm"),
        P(None, None, "mp"),
        P("mp", None),
        P(None, "mp"),
        P("mp", None),
    )
    out_specs = P("tm", None, "mp")
    run = functools.partial(body, mesh.shape["mp"], mesh.shape["tm"])
    return jax.shard_map(run, mesh=mesh, in_specs=in_specs, out_specs=out_specs, check_vma=False)
```

time: 582 us -> 468 us (0.80); the launches traced: 575 us -> 467 us
  Pallas kernels: 0 us -> 207 us
  waiting for transfers between devices: 311 us -> 142 us
  local copies, waits for them, and re-layouts: 107 us -> 53.7 us
  matrix products: 61.1 us -> 14.3 us
  other arithmetic: 47.5 us -> 3.63 us
    pallas_call x0 -> x2, Pallas kernels: none -> 207 us  [the longest x1 190 us: tail(): pl.pallas_call(functools.partial(tail_kernel, n, CHUNKS), out_shape=jax.S...]
    reduce_scatter x2 -> x0, waiting for transfers between devices: 169 us -> none  [the longest x1 85.2 us: dense_tail(): lax.psum_scatter(attn_term.astype(jnp.bfloat16), 'mp', scatter_dimension=...]
    all_gather x2 -> x1, waiting for transfers between devices: 112 us -> 62.8 us  [body(): full_rows = lax.all_gather(frame_rows, 'mp', axis=1, tiled=True)]
    all_to_all x3, waiting for transfers between devices: 29.1 us -> 78.1 us  [the longest x2 43.4 us: to_patches(): return lax.all_to_all(blocks, 'tm', split_axis=0, concat_axis=0)]
    dot_general x7 -> x1, matrix products: 61.1 us -> 14.3 us  [body(): jnp.dot(unit_rows(full_rows), joined_weight, preferred_element_type=jnp.f...]
    convert_element_type x5 -> x0, local copies, waits for them, and re-layouts: 25.9 us -> none  [the longest x4 25.5 us: unit_heads(): widened = tensor.astype(jnp.float32)]
    convert_element_type x5 -> x0, other arithmetic: 22.5 us -> none  [the longest x2 14.5 us: unit_heads(): return (widened * lax.rsqrt(mean_square + 1e-06)).astype(jnp.bfloat16)]
    reduce_sum x5 -> x1, other arithmetic: 20.3 us -> 3.47 us  [unit_rows(): mean_square = jnp.mean(widened * widened, axis=-1, keepdims=True)]
  transfers between devices with their start and end apart: 7 -> 4, of which waited for: 5 -> 3; matrix products, arithmetic and copies ran while one was open for 22% -> 14% of each run, Pallas kernels for 0% -> 0%
where the time goes in v1:
time: 468 us; the launch traced here: 467 us
  Pallas kernels  207 us (44%)
  waiting for transfers between devices  142 us (30%)
  local copies, waits for them, and re-layouts  53.7 us (11%)
  blocking collectives  19.2 us (4%)
  matrix products  14.3 us (3%)
  starting transfers between devices  13.7 us (3%)
  between operations  13.5 us (3%)
    pallas_call x1, Pallas kernels, tail(): pl.pallas_call(functools.partial(tail_kernel, n, CHUNKS), out_shape=jax.S...  190 us
    all_gather x1, waiting for transfers between devices, body(): full_rows = lax.all_gather(frame_rows, 'mp', axis=1, tiled=True)  62.8 us
    all_to_all x2, waiting for transfers between devices, to_patches(): return lax.all_to_all(blocks, 'tm', split_axis=0, concat_axis=0)  43.4 us
    unnamed x10, local copies, waits for them, and re-layouts  35.6 us
    all_to_all x1, waiting for transfers between devices, body(): lax.all_to_all(projected.transpose(1, 0, 2, 3), 'tm', split_axis=0, conca...  34.7 us
    all_to_all x1, blocking collectives, body(): returned = lax.all_to_all(heads_out, 'tm', split_axis=0, concat_axis=0)  19.2 us
    pallas_call x1, Pallas kernels, attend(): pl.pallas_call(functools.partial(attend_kernel, patches), grid=(patch_cou...  16.8 us
    dot_general x1, matrix products, body(): jnp.dot(unit_rows(full_rows), joined_weight, preferred_element_type=jnp.f...  14.3 us
  transfers between devices with their start and end apart: 4, of which 3 were waited for; matrix products, arithmetic and copies ran while one was open for 14% of the time, Pallas kernels for 0%

profile of v1, /device:TPU:0, one launch (start us, length us, event | category | flops | bytes accessed | tf_op | source)
XLA Modules:
  0.0 466.8 jit_solution(12277091754483465162)
XLA Ops:
  6.5 0.0 all-gather.2.cloned.1.call-start
  6.5 0.7 all-gather.2.cloned.1.call-update
  7.3 7.1 %copy.22 = bf16[8,384,768]{2,0,1:T(8,128)(2,1)} copy(bf16[8,384,768]{2,1,0:T(8,128)(2,1)} %param.10) | data formatting | bytes 9437184 | tf_op args[1]
  14.4 5.2 %all-to-all-start.1 = ((bf16[8,48,8,768]{3,2,1,0:T(8,128)(2,1)}), bf16[8,48,8,768]{3,2,1,0:T(8,128)(2,1)}, u32[]{:S(2)}, u32[]{:S(2)}) async-start(bf16[8,48,8,768]{3,2,1,0:T(8,128)(2,1)} %bitcast.26), calls=%async_computation.1 | async-start | bytes 9437184 | tf_op jit(solution)/shard_map/all_to_all | solution.py:337
  19.5 18.7 %copy.19 = bf16[3072,3,768]{0,2,1:T(8,128)(2,1)} copy(bf16[3072,3,768]{2,0,1:T(8,128)(2,1)} %param.14) | data formatting | bytes 28311552 | tf_op args[5]
  38.3 62.8 %all-gather.2.cloned.1.call-done = bf16[768,3072]{1,0:T(8,128)(2,1)} async-done(((bf16[768,768]{1,0:T(8,128)(2,1)}), bf16[768,3072]{1,0:T(8,128)(2,1)}) %all-gather.2.cloned.1.call-update) | async-done | bytes 4718608 | tf_op jit(solution)/shard_map/all_gather | solution.py:349
  101.1 0.0 copy-start.1
  101.1 3.5 fusion
  104.6 0.3 copy-done.1
  104.8 14.3 %convolution_convert_fusion = bf16[768,2304]{1,0:T(8,128)(2,1)S(1)} fusion(bf16[3072,2304]{0,1:T(8,128)(2,1)} %bitcast.28, bf16[768,3072]{1,0:T(8,128)(2,1)S(1)} %copy-done.1, f32[768]{0:T(1024)S(1)} %add_rsqrt_fusion), kind=kOutput, calls=%fused_computation.4 | convolution fusion | flops 10880483328 | bytes 22416384 | tf_op jit(solution)/shard_map/dot_general | solution.py:352
  119.2 5.4 %copy.28 = bf16[2,8,48,2304]{3,0,2,1:T(2,128)(2,1)} copy(bf16[2,8,48,2304]{3,2,1,0:T(8,128)(2,1)S(1)} %bitcast.36) | data formatting | bytes 7077888 | tf_op jit(solution)/shard_map/reshape | solution.py:353
  124.6 0.0 all-to-all-done.1.keys_ref
  124.6 3.8 all-to-all-start
  128.4 7.1 %copy.23 = bf16[8,384,768]{2,0,1:T(8,128)(2,1)} copy(bf16[8,384,768]{2,1,0:T(8,128)(2,1)} %param.11) | data formatting | bytes 9437184 | tf_op args[2]
  135.6 34.7 %all-to-all-done = bf16[8,2,48,2304]{3,1,2,0:T(2,128)(2,1)S(1)} async-done(((bf16[8,2,48,2304]{3,1,2,0:T(2,128)(2,1)}), bf16[8,2,48,2304]{3,1,2,0:T(2,128)(2,1)S(1)}, u32[]{:S(2)}, u32[]{:S(2)}) %all-to-all-start) | async-done | bytes 3538976 | tf_op jit(solution)/shard_map/all_to_all | solution.py:354
  170.3 0.0 copy-start.2
  170.3 4.7 %all-to-all-start.2 = ((bf16[8,48,8,768]{3,2,1,0:T(8,128)(2,1)}), bf16[8,48,8,768]{3,2,1,0:T(8,128)(2,1)}, u32[]{:S(2)}, u32[]{:S(2)}) async-start(bf16[8,48,8,768]{3,2,1,0:T(8,128)(2,1)} %bitcast.27), calls=%async_computation.2 | async-start | bytes 9437184 | tf_op jit(solution)/shard_map/all_to_all | solution.py:337
  175.0 0.0 copy-done.2
  175.1 0.1 broadcast_compare_fusion
  175.1 0.1 pad_convert_fusion
  175.2 4.2 copy.21
  179.4 0.0 copy-start
  179.4 7.0 %reshape.38 = bf16[16,48,2304]{2,0,1:T(8,128)(2,1)S(1)} reshape(bf16[8,2,48,2304]{3,1,0,2:T(2,128)(2,1)} %copy.21) | data formatting | bytes 7077888 | tf_op jit(solution)/shard_map/reshape | solution.py:355
  186.4 43.3 %all-to-all-done.2.values_ref = bf16[8,48,8,768]{3,2,1,0:T(8,128)(2,1)} async-done(((bf16[8,48,8,768]{3,2,1,0:T(8,128)(2,1)}), bf16[8,48,8,768]{3,2,1,0:T(8,128)(2,1)}, u32[]{:S(2)}, u32[]{:S(2)}) %all-to-all-start.2) | async-done | bytes 4718624 | tf_op jit(solution)/shard_map/all_to_all | solution.py:337
  229.8 0.0 copy-done
  229.8 16.8 %attend.1 = bf16[48,16,768]{2,1,0:T(8,128)(2,1)S(1)} custom-call(s32[48]{0:T(128)S(1)} %copy-done, f32[96,80]{1,0:T(8,128)S(1)} %bitcast.25, bf16[48,16,2304]{2,1,0:T(8,128)(2,1)S(1)} %bitcast.23, bf16[8,48,8,768]{3,2,1,0:T(8,128)(2,1)} %all-to-all-done.1.keys_ref, bf16[8,48,8,768]{3,2,1,0:T(8,128)(2,1)} %all-to-all-done.2.values_ref), custom_call_target="tpu_custom_call" | custom-call | tf_op jit(solution)/shard_map/attend/pallas_call | solution.py:68
  246.6 0.3 copy.26
  246.9 19.2 %all_to_all.20 = bf16[8,2,48,768]{3,2,1,0:T(8,128)(2,1)S(1)} all-to-all(bf16[8,2,48,768]{3,2,1,0:T(8,128)(2,1)S(1)} %bitcast.34), channel_id=1, replica_groups=mesh['tm'=8,'mp'=4] {'tm'}, dimensions={0} | all-to-all | bytes 2359296 | tf_op jit(solution)/shard_map/all_to_all | solution.py:358
  266.1 1.1 copy.25
  267.2 190.4 %tail.1 = bf16[8,96,768]{2,1,0:T(8,128)(2,1)} custom-call(bf16[8,96,768]{2,1,0:T(8,128)(2,1)} %bitcast.32, bf16[8,96,768]{2,1,0:T(8,128)(2,1)} %bitcast.31, bf16[768,3072]{1,0:T(8,128)(2,1)} %out_w_hbm.1, bf16[3072,1536]{1,0:T(8,128)(2,1)} %up_w_hbm.1, bf16[1536,3072]{1,0:T(8,128)(2,1)} %down_w_hbm.1), custom_call_target="tpu_custom_call" | custom-call | tf_op jit(solution)/shard_map/tail/pallas_call | solution.py:307
  457.5 2.4 copy.30
  (2 shorter events, 0.0 us)
Async XLA Ops:
  6.5 94.5 %all-gather.2.cloned.1.call-start = ((), (), s32[]{:S(2)}) async-start(), calls=%async_computation.4 | async-start | bytes 5898240 | tf_op jit(solution)/shard_map/all_gather | solution.py:349
  14.4 110.2 %all-to-all-start.1 = ((bf16[8,48,8,768]{3,2,1,0:T(8,128)(2,1)}), bf16[8,48,8,768]{3,2,1,0:T(8,128)(2,1)}, u32[]{:S(2)}, u32[]{:S(2)}) async-start(bf16[8,48,8,768]{3,2,1,0:T(8,128)(2,1)} %bitcast.26), calls=%async_computation.1 | async-start | bytes 9437184 | tf_op jit(solution)/shard_map/all_to_all | solution.py:337
  101.1 3.8 copy-start.1
  124.6 45.7 %all-to-all-start = ((bf16[8,2,48,2304]{3,1,2,0:T(2,128)(2,1)}), bf16[8,2,48,2304]{3,1,2,0:T(2,128)(2,1)S(1)}, u32[]{:S(2)}, u32[]{:S(2)}) async-start(bf16[8,2,48,2304]{3,1,2,0:T(2,128)(2,1)} %bitcast.29), calls=%async_computation | async-start | bytes 7077888 | tf_op jit(solution)/shard_map/all_to_all | solution.py:354
  170.3 4.7 %copy-start.2 = (s32[16]{0:T(128)S(1)}, s32[16]{0:T(128)}, u32[]{:S(2)}) copy-start(s32[16]{0:T(128)} %param.12) | copy-start | bytes 196
  170.3 59.5 %all-to-all-start.2 = ((bf16[8,48,8,768]{3,2,1,0:T(8,128)(2,1)}), bf16[8,48,8,768]{3,2,1,0:T(8,128)(2,1)}, u32[]{:S(2)}, u32[]{:S(2)}) async-start(bf16[8,48,8,768]{3,2,1,0:T(8,128)(2,1)} %bitcast.27), calls=%async_computation.2 | async-start | bytes 9437184 | tf_op jit(solution)/shard_map/all_to_all | solution.py:337
  179.4 50.4 %copy-start = (s32[48]{0:T(128)S(1)}, s32[48]{0:T(128)}, u32[]{:S(2)}) copy-start(s32[48]{0:T(128)} %counts_ref.1) | copy-start | bytes 580
Sparse Core Ops, SparseCore 0:
  8.9 92.0 all-gather.1

commit v2 on v0

v2 whole, which is shorter than its diff:
```python
import functools
import math

import jax
import jax.numpy as jnp
from jax import lax
from jax.experimental import pallas as pl
from jax.experimental.pallas import tpu as pltpu
from jax.sharding import PartitionSpec as P

HD = 128
GROUP = 8
MESH = pl.DeviceIdType.MESH


def unit_rows(tensor):
    widened = tensor.astype(jnp.float32)
    mean_square = jnp.mean(widened * widened, axis=-1, keepdims=True)
    return (widened * lax.rsqrt(mean_square + 1e-06)).astype(jnp.bfloat16)


def block_kernel(
    n, peers, chunks, slab,
    states_hbm, keys_hbm, values_hbm, mask_ref, qkv_hbm, out_w_hbm, up_w_hbm, down_w_hbm,
    result_ref, keys_land, values_land,
    qkv_w, out_w, up_w, down_w, keys, values, fresh, returned, terms, landed, middle,
    local_sem, qkv_sem, own_sem, cache_send, cache_recv, fresh_send, fresh_recv, heads_send, heads_recv,
    sum_send, sum_recv, right_send, left_send, gather_recv,
):
    me = lax.axis_index("mp")
    here = lax.axis_index("tm")
    rows, width = returned.shape[1:]
    last = n - 1
    at_qkv = last
    at_attend = last + 1
    at_out = last + 2
    at_ffn = at_out + 2 * last

    def peer(k):
        return lax.rem(here + k, peers)

    states_load = pltpu.make_async_copy(states_hbm, middle.at[:, me], local_sem.at[0])
    states_load.start()
    caches = ((0, keys_hbm, keys_land, keys), (1, values_hbm, values_land, values))
    weight_loads = [
        pltpu.make_async_copy(src, dst, local_sem.at[k])
        for k, src, dst in ((1, out_w_hbm, out_w), (2, up_w_hbm, up_w), (3, down_w_hbm, down_w))
    ]

    def qkv_load(j, slot):
        return pltpu.make_async_copy(qkv_hbm.at[j], qkv_w.at[slot], qkv_sem.at[slot])

    qkv_load(0, 0).start()
    qkv_load(1, 1).start()

    barrier = pltpu.get_barrier_semaphore()
    for k in range(1, peers):
        pl.semaphore_signal(barrier, inc=1, device_id={"tm": peer(k)}, device_id_type=MESH)

    @pl.when(me > 0)
    def _():
        pl.semaphore_signal(barrier, inc=1, device_id={"mp": me - 1}, device_id_type=MESH)

    @pl.when(me < last)
    def _():
        pl.semaphore_signal(barrier, inc=1, device_id={"mp": me + 1}, device_id_type=MESH)

    @pl.when((me > 0) & (me < last))
    def _():
        pl.semaphore_wait(barrier, peers + 1)

    @pl.when((me == 0) | (me == last))
    def _():
        pl.semaphore_wait(barrier, peers)

    def cache_copy(kind, src, land, c, to, origin):
        return pltpu.make_async_remote_copy(
            src_ref=src.at[:, to * chunks + c],
            dst_ref=land.at[c, origin],
            send_sem=cache_send.at[c, kind, to],
            recv_sem=cache_recv.at[c, kind, origin],
            device_id={"tm": to},
            device_id_type=MESH,
        )

    def own_cache(kind, src, land, c):
        return pltpu.make_async_copy(
            src.at[:, here * chunks + c], land.at[c, here], own_sem.at[c, kind]
        )

    def send_cache(c):
        for kind, src, land, _ in caches:
            for k in range(1, peers):
                cache_copy(kind, src, land, c, peer(k), here).start()
            own_cache(kind, src, land, c).start()

    def slab_of(device):
        return pl.ds(pl.multiple_of(device * slab, slab), slab)

    def fresh_copy(c, to, origin):
        return pltpu.make_async_remote_copy(
            src_ref=terms.at[c, pl.ds(0, 3), slab_of(to)],
            dst_ref=fresh.at[c, :, slab_of(origin)],
            send_sem=fresh_send.at[c, to],
            recv_sem=fresh_recv.at[c, origin],
            device_id={"tm": to},
            device_id_type=MESH,
        )

    def own_fresh(c):
        return pltpu.make_async_copy(
            terms.at[c, pl.ds(0, 3), slab_of(here)], fresh.at[c, :, slab_of(here)], own_sem.at[c, 2]
        )

    def heads_copy(c, to, origin):
        return pltpu.make_async_remote_copy(
            src_ref=terms.at[c, last, slab_of(to)],
            dst_ref=returned.at[c, slab_of(origin)],
            send_sem=heads_send.at[c, to],
            recv_sem=heads_recv.at[c, origin],
            device_id={"tm": to},
            device_id_type=MESH,
        )

    def own_heads(c):
        return pltpu.make_async_copy(
            terms.at[c, last, slab_of(here)], returned.at[c, slab_of(here)], own_sem.at[c, 3]
        )

    def sum_copy(c, d, slot, target):
        return pltpu.make_async_remote_copy(
            src_ref=terms.at[c, d],
            dst_ref=landed.at[c, slot],
            send_sem=sum_send.at[c, d],
            recv_sem=sum_recv.at[c, slot],
            device_id={"mp": target},
            device_id_type=MESH,
        )

    def gather_copy(c, d, send_sem, target):
        return pltpu.make_async_remote_copy(
            src_ref=middle.at[c, d],
            dst_ref=middle.at[c, d],
            send_sem=send_sem.at[c, d],
            recv_sem=gather_recv.at[c, d],
            device_id={"mp": target},
            device_id_type=MESH,
        )

    def active(c):
        return (c >= 0) & (c < chunks)

    def add_landed(c, d, slot):
        sum_copy(c, d, slot, me).wait_recv()
        terms[c, d] = (
            terms[c, d].astype(jnp.float32) + landed[c, slot].astype(jnp.float32)
        ).astype(jnp.bfloat16)

    def sum_right(tick):
        c = tick - me
        for d in range(last, 0, -1):
            @pl.when(active(c) & (me < d))
            def _():
                @pl.when(me > 0)
                def _():
                    add_landed(c, d, d)

                sum_copy(c, d, d, me + 1).start()

    def sum_left(tick):
        c = tick - (last - me)
        for d in range(last):
            @pl.when(active(c) & (me > d))
            def _():
                @pl.when(me < last)
                def _():
                    add_landed(c, d, d)

                @pl.when(me - 1 == d)
                def _():
                    sum_copy(c, d, n, me - 1).start()

                @pl.when(me - 1 > d)
                def _():
                    sum_copy(c, d, d, me - 1).start()

    def wait_gather_sends(c):
        for d in range(n):
            @pl.when((d <= me) & (me < last))
            def _():
                gather_copy(c, d, right_send, me).wait_send()

            @pl.when((d >= me) & (me > 0))
            def _():
                gather_copy(c, d, left_send, me).wait_send()

    def gather_own(c):
        @pl.when(me < last)
        def _():
            gather_copy(c, me, right_send, me + 1).start()

        @pl.when(me > 0)
        def _():
            gather_copy(c, me, left_send, me - 1).start()

    def gather_hops(tick):
        for h in range(last, 0, -1):
            c = tick - h

            @pl.when(active(c) & (me - h >= 0))
            def _():
                gather_copy(c, me - h, right_send, me).wait_recv()

                @pl.when(me < last)
                def _():
                    gather_copy(c, me - h, right_send, me + 1).start()

            @pl.when(active(c) & (me + h <= last))
            def _():
                gather_copy(c, me + h, left_send, me).wait_recv()

                @pl.when(me > 0)
                def _():
                    gather_copy(c, me + h, left_send, me - 1).start()

    def normed_blocks(c):
        squares = jnp.zeros((rows, 1), jnp.float32)
        for d in range(n):
            block = middle[c, d].astype(jnp.float32)
            squares = squares + jnp.sum(block * block, axis=-1, keepdims=True)
        factor = lax.rsqrt(squares / (n * width) + 1e-06)
        return [(middle[c, d].astype(jnp.float32) * factor).astype(jnp.bfloat16) for d in range(n)]

    def product(blocks, weight):
        total = None
        for d in range(n):
            part = jnp.dot(
                blocks[d], weight[d * width : (d + 1) * width, :], preferred_element_type=jnp.float32
            )
            total = part if total is None else total + part
        return total

    def sum_end(c):
        @pl.when(me > 0)
        def _():
            sum_copy(c, me, me, me).wait_recv()

        @pl.when(me < last)
        def _():
            sum_copy(c, me, n, me).wait_recv()

        zero = jnp.zeros((rows, width), jnp.float32)
        from_left = jnp.where(me > 0, landed[c, me].astype(jnp.float32), zero)
        from_right = jnp.where(me < last, landed[c, n].astype(jnp.float32), zero)
        return terms[c, me].astype(jnp.float32) + from_left + from_right

    def wait_sum_sends(c):
        for d in range(n):
            @pl.when(me != d)
            def _():
                sum_copy(c, d, d, me).wait_send()

    def project(c):
        blocks = normed_blocks(c)
        for j in range(3):
            slot = lax.rem(c * 3 + j, 2)
            qkv_load(j, slot).wait()
            terms[c, j] = product(blocks, qkv_w.at[slot]).astype(jnp.bfloat16)

            @pl.when(c * 3 + j + 2 < 3 * chunks)
            def _():
                qkv_load((j + 2) % 3, slot).start()

        for k in range(1, peers):
            fresh_copy(c, peer(k), here).start()
        own_fresh(c).start()

    def attend(c):
        for kind, src, land, held in caches:
            for k in range(1, peers):
                cache_copy(kind, src, land, c, here, peer(k)).wait_recv()
            own_cache(kind, src, land, c).wait()
            pltpu.make_async_copy(land.at[c], held, local_sem.at[4 + kind]).start()
        for k in range(1, peers):
            fresh_copy(c, here, peer(k)).wait_recv()
        own_fresh(c).wait()
        for kind, _, land, held in caches:
            pltpu.make_async_copy(land.at[c], held, local_sem.at[4 + kind]).wait()
        mask = mask_ref[c].astype(jnp.float32)
        scale = 1.0 / math.sqrt(HD)
        for h in range(width // HD):
            at = slice(h * HD, (h + 1) * HD)
            old_keys = keys[:, :, :, at].astype(jnp.float32).reshape(-1, HD)
            old_values = values[:, :, :, at].astype(jnp.float32).reshape(-1, HD).astype(jnp.bfloat16)
            all_keys = jnp.concatenate([unit_rows(old_keys), unit_rows(fresh[c, 1, :, at])], axis=0)
            all_values = jnp.concatenate([old_values, fresh[c, 2, :, at]], axis=0)
            scores = lax.dot_general(
                unit_rows(fresh[c, 0, :, at]), all_keys, (((1,), (1,)), ((), ())),
                preferred_element_type=jnp.float32,
            )
            raised = jnp.exp(scores * scale) * mask
            weights = (raised / jnp.sum(raised, axis=-1, keepdims=True)).astype(jnp.bfloat16)
            terms[c, last, :, at] = jnp.dot(
                weights, all_values, preferred_element_type=jnp.float32
            ).astype(jnp.bfloat16)
        for k in range(1, peers):
            heads_copy(c, peer(k), here).start()
        own_heads(c).start()

    def project_out(c):
        for k in range(1, peers):
            heads_copy(c, here, peer(k)).wait_recv()
            heads_copy(c, peer(k), here).wait_send()
            fresh_copy(c, peer(k), here).wait_send()
        own_heads(c).wait()
        wait_gather_sends(c)
        block = returned[c]
        for d in range(n):
            terms[c, d] = jnp.dot(
                block, out_w[:, d * width : (d + 1) * width], preferred_element_type=jnp.float32
            ).astype(jnp.bfloat16)

    def feed_forward(c):
        wait_sum_sends(c)
        hidden = jax.nn.gelu(product(normed_blocks(c), up_w)).astype(jnp.bfloat16)
        for d in range(n):
            terms[c, d] = jnp.dot(
                hidden, down_w[:, d * width : (d + 1) * width], preferred_element_type=jnp.float32
            ).astype(jnp.bfloat16)

    def step(tick, carry):
        @pl.when((tick >= 2) & (tick < chunks))
        def _():
            send_cache(tick)

        @pl.when(tick < chunks)
        def _():
            gather_own(tick)

        gather_hops(tick)

        @pl.when(active(tick - at_qkv))
        def _():
            project(tick - at_qkv)

        gather_hops(tick - at_out - last)

        @pl.when(tick == at_out)
        def _():
            weight_loads[0].wait()

        @pl.when(active(tick - at_out))
        def _():
            project_out(tick - at_out)

        sum_right(tick - at_out)
        sum_left(tick - at_out)
        c_mid = tick - at_out - last

        @pl.when(active(c_mid))
        def _():
            total = sum_end(c_mid)
            middle[c_mid, me] = (middle[c_mid, me].astype(jnp.float32) + total).astype(jnp.bfloat16)
            gather_own(c_mid)

        @pl.when(tick == at_ffn)
        def _():
            weight_loads[1].wait()
            weight_loads[2].wait()

        @pl.when(active(tick - at_ffn))
        def _():
            feed_forward(tick - at_ffn)

        sum_right(tick - at_ffn)
        sum_left(tick - at_ffn)
        c_end = tick - at_ffn - last

        @pl.when(active(c_end))
        def _():
            total = sum_end(c_end)
            result_ref[c_end] = (middle[c_end, me].astype(jnp.float32) + total).astype(jnp.bfloat16)

        @pl.when(active(tick - at_attend))
        def _():
            attend(tick - at_attend)

        return carry

    states_load.wait()
    for c in range(min(2, chunks)):
        send_cache(c)
    for load in weight_loads:
        load.start()
    lax.fori_loop(0, chunks + at_ffn + last, step, 0)

    def drain(c, carry):
        wait_sum_sends(c)
        wait_gather_sends(c)
        for kind, src, land, _ in caches:
            for k in range(1, peers):
                cache_copy(kind, src, land, c, peer(k), here).wait_send()
        return carry

    lax.fori_loop(0, chunks, drain, 0)


def body(
    n, peers,
    states, key_cache, value_cache, frame_times, valid_counts,
    qkv_weight, out_weight, up_weight, down_weight,
):
    frames, patch_count, width = states.shape
    share = key_cache.shape[0]
    cache = share * peers
    chunks = patch_count // peers // GROUP
    slab = frames * GROUP
    rows = peers * slab

    row = jnp.arange(rows, dtype=jnp.int32)
    row_patch, row_frame = row % GROUP, row // GROUP
    column = jnp.arange(cache * GROUP, dtype=jnp.int32)
    column_patch, column_frame = column % GROUP, column // GROUP
    limits = (cache - valid_counts.reshape(chunks, GROUP))[:, row_patch]
    cached_ok = (row_patch[:, None] == column_patch[None, :])[None] & (
        column_frame[None, None, :] >= limits[:, :, None]
    )
    times = frame_times[row_frame]
    fresh_ok = (row_patch[:, None] == row_patch[None, :]) & (times[None, :] <= times[:, None])
    fresh_ok = jnp.broadcast_to(fresh_ok[None], (chunks, rows, rows))
    mask = jnp.concatenate([cached_ok, fresh_ok], axis=2).astype(jnp.bfloat16)

    arranged = states.reshape(frames, peers, chunks, GROUP, width).transpose(2, 1, 0, 3, 4)
    arranged = arranged.reshape(chunks, rows, width)
    keys = key_cache.reshape(share, peers * chunks, GROUP, width)
    values = value_cache.reshape(share, peers * chunks, GROUP, width)
    qkv = qkv_weight.transpose(1, 0, 2)

    vmem = pl.BlockSpec(memory_space=pltpu.VMEM)
    hbm = pl.BlockSpec(memory_space=pl.ANY)
    land = jax.ShapeDtypeStruct((chunks, peers, share, GROUP, width), jnp.bfloat16)
    bf16 = jnp.bfloat16
    dma = pltpu.SemaphoreType.DMA
    result, _, _ = pl.pallas_call(
        functools.partial(block_kernel, n, peers, chunks, slab),
        out_shape=(jax.ShapeDtypeStruct(arranged.shape, bf16), land, land),
        in_specs=[hbm, hbm, hbm, vmem, hbm, hbm, hbm, hbm],
        out_specs=(vmem, hbm, hbm),
        scratch_shapes=[
            pltpu.VMEM((2,) + qkv.shape[1:], bf16),
            pltpu.VMEM(out_weight.shape, bf16),
            pltpu.VMEM(up_weight.shape, bf16),
            pltpu.VMEM(down_weight.shape, bf16),
            pltpu.VMEM(land.shape[1:], bf16),
            pltpu.VMEM(land.shape[1:], bf16),
            pltpu.VMEM((chunks, 3, rows, width), bf16),
            pltpu.VMEM((chunks, rows, width), bf16),
            pltpu.VMEM((chunks, n, rows, width), bf16),
            pltpu.VMEM((chunks, n + 1, rows, width), bf16),
            pltpu.VMEM((chunks, n, rows, width), bf16),
            dma((6,)),
            dma((2,)),
            dma((chunks, 4)),
            dma((chunks, 2, peers)),
            dma((chunks, 2, peers)),
            dma((chunks, peers)),
            dma((chunks, peers)),
            dma((chunks, peers)),
            dma((chunks, peers)),
            dma((chunks, n)),
            dma((chunks, n + 1)),
            dma((chunks, n)),
            dma((chunks, n)),
            dma((chunks, n)),
        ],
        compiler_params=pltpu.CompilerParams(
            collective_id=1, has_side_effects=True, vmem_limit_bytes=62 * 2**20
        ),
        name="block",
    )(arranged, keys, values, mask, qkv, out_weight, up_weight, down_weight)
    result = result.reshape(chunks, peers, frames, GROUP, width).transpose(2, 1, 0, 3, 4)
    return result.reshape(states.shape)


def solution(mesh):
    in_specs = (
        P("tm", None, "mp"),
        P("tm", None, "mp"),
        P("tm", None, "mp"),
        P(),
        P("tm"),
        P(None, None, "mp"),
        P("mp", None),
        P(None, "mp"),
        P("mp", None),
    )
    out_specs = P("tm", None, "mp")
    run = functools.partial(body, mesh.shape["mp"], mesh.shape["tm"])
    return jax.shard_map(run, mesh=mesh, in_specs=in_specs, out_specs=out_specs, check_vma=False)
```

time: 582 us -> 335 us (0.58); the launches traced: 575 us -> 334 us
  Pallas kernels: 0 us -> 314 us
  waiting for transfers between devices: 311 us -> 0 us
  local copies, waits for them, and re-layouts: 107 us -> 7.58 us
  matrix products: 61.1 us -> 0 us
  other arithmetic: 47.5 us -> 12.3 us
  blocking collectives: 20.7 us -> 0 us
  starting transfers between devices: 13.9 us -> 0 us
  between operations: 13.5 us -> 0.06 us
    pallas_call x0 -> x1, Pallas kernels: none -> 314 us  [body(): pl.pallas_call(functools.partial(block_kernel, n, peers, chunks, slab), o...]
    reduce_scatter x2 -> x0, waiting for transfers between devices: 169 us -> none  [the longest x1 85.2 us: dense_tail(): lax.psum_scatter(attn_term.astype(jnp.bfloat16), 'mp', scatter_dimension=...]
    all_gather x2 -> x0, waiting for transfers between devices: 112 us -> none  [normed_product(): full_rows = lax.all_gather(token_rows, 'mp', axis=1, tiled=True)]
    dot_general x7 -> x0, matrix products: 61.1 us -> none  [the longest x1 24.4 us: dense_tail(): ffn_term = jnp.dot(hidden, down_weight, preferred_element_type=jnp.float32)]
    unnamed x19 -> x0, local copies, waits for them, and re-layouts: 33.6 us -> none
    all_to_all x3 -> x0, waiting for transfers between devices: 29.1 us -> none  [the longest x1 29.1 us: body(): lax.all_to_all(key_cache, 'tm', split_axis=1, concat_axis=0, tiled=True)]
    convert_element_type x5 -> x0, local copies, waits for them, and re-layouts: 25.9 us -> none  [the longest x4 25.5 us: unit_heads(): widened = tensor.astype(jnp.float32)]
    reshape x4 -> x1, local copies, waits for them, and re-layouts: 27.1 us -> 2.39 us  [body(): states.reshape(frames, peers, chunks, GROUP, width).transpose(2, 1, 0, 3, 4)]
  transfers between devices with their start and end apart: 7 -> 0, of which waited for: 5 -> 0; matrix products, arithmetic and copies ran while one was open for 22% -> 0% of each run, Pallas kernels for 0% -> 0%
where the time goes in v2:
time: 335 us; the launch traced here: 334 us
  Pallas kernels  314 us (94%)
  other arithmetic  12.3 us (4%)
  local copies, waits for them, and re-layouts  7.58 us (2%)
    pallas_call x1, Pallas kernels, body(): pl.pallas_call(functools.partial(block_kernel, n, peers, chunks, slab), o...  314 us
    gather x1, other arithmetic, body(): times = frame_times[row_frame]  9.95 us

profile of v2, /device:TPU:0, one launch (start us, length us, event | category | flops | bytes accessed | tf_op | source)
XLA Modules:
  0.0 334.2 jit_solution(16605171786026526128)
XLA Ops:
  0.0 0.7 broadcast_subtract_fusion
  0.7 0.1 sub.24
  0.8 0.1 copy.11
  0.8 1.9 fusion.7
  2.8 10.0 %bitcast_select_fusion.8 = (s32[128]{0:T(128)S(1)}, s32[128]{0:T(128)S(1)}) fusion(s32[]{:T(128)} %bitcast.25, s32[]{:T(128)} %bitcast.26, s32[]{:T(128)} %bitcast.27, s32[]{:T(128)} %bitcast.28, s32[]{:T(128)} %bitcast.29, s32[]{:T(128)} %bitcast.31, s32[]{:T(128)} %bitcast.30, s32[]{:T(128)} %bitcast.8, s32[]{:T(128)} %bitcast.10, s32[]{:T(128)} %bitcast.12, ...), kind=kLoop, calls=%fused_computation.26 | loop fusion | flops 6016 | bytes 1088 | tf_op jit(solution)/shard_map/gather | solution.py:428
  12.7 0.1 compare_and_fusion.1
  12.9 0.6 gather_fusion
  13.5 0.1 copy.12
  13.6 0.1 broadcast_compare_fusion
  13.7 0.3 compare_and_fusion
  14.1 1.1 add_convert_fusion.mask_ref
  15.2 2.4 copy.10
  17.6 314.3 %block.1 = (bf16[6,128,768]{2,1,0:T(8,128)(2,1)}, bf16[6,8,8,8,768]{4,3,2,1,0:T(8,128)(2,1)}, bf16[6,8,8,8,768]{4,3,2,1,0:T(8,128)(2,1)}) custom-call(bf16[6,128,768]{2,1,0:T(8,128)(2,1)} %bitcast.71, bf16[8,48,8,768]{3,2,1,0:T(8,128)(2,1)} %bitcast.69, bf16[8,48,8,768]{3,2,1,0:T(8,128)(2,1)} %bitcast.70, bf16[6,128,640]{2,1,0:T(8,128)(2,1)} %add_convert_fusion.mask_ref, ...), custom_call_target="tpu_custom_call" | custom-call | tf_op jit(solution)/shard_map/block/pallas_call | solution.py:444
  331.9 2.4 copy.13
  (5 shorter events, 0.0 us)

commit v3 on v2

--- a/solution.py
+++ b/solution.py
@@ -418,14 +418,15 @@
     rows = peers * slab
 
     row = jnp.arange(rows, dtype=jnp.int32)
-    row_patch, row_frame = row % GROUP, row // GROUP
+    row_patch = row % GROUP
     column = jnp.arange(cache * GROUP, dtype=jnp.int32)
     column_patch, column_frame = column % GROUP, column // GROUP
-    limits = (cache - valid_counts.reshape(chunks, GROUP))[:, row_patch]
+    limits = cache - valid_counts.reshape(chunks, 1, GROUP)
+    limits = jnp.broadcast_to(limits, (chunks, rows // GROUP, GROUP)).reshape(chunks, rows)
     cached_ok = (row_patch[:, None] == column_patch[None, :])[None] & (
         column_frame[None, None, :] >= limits[:, :, None]
     )
-    times = frame_times[row_frame]
+    times = jnp.broadcast_to(frame_times[:, None], (rows // GROUP, GROUP)).reshape(rows)
     fresh_ok = (row_patch[:, None] == row_patch[None, :]) & (times[None, :] <= times[:, None])
     fresh_ok = jnp.broadcast_to(fresh_ok[None], (chunks, rows, rows))
     mask = jnp.concatenate([cached_ok, fresh_ok], axis=2).astype(jnp.bfloat16)

time: 335 us -> 323 us (0.964)
  other arithmetic: 12.3 us -> 2.35 us
    gather x2 -> x0, other arithmetic: 9.96 us -> none  [the longest x1 9.95 us: body(): times = frame_times[row_frame]]
where the time goes in v3:
time: 323 us; the launch traced here: 322 us
  Pallas kernels  314 us (97%)
  local copies, waits for them, and re-layouts  5.76 us (2%)
    pallas_call x1, Pallas kernels, body(): pl.pallas_call(functools.partial(block_kernel, n, peers, chunks, slab), o...  314 us

profile of v3, /device:TPU:0, one launch (start us, length us, event | category | flops | bytes accessed | tf_op | source)
XLA Modules:
  0.0 322.5 jit_solution(15765831022363034414)
XLA Ops:
  0.0 0.7 broadcast_subtract_fusion
  0.7 0.1 sub.23
  0.7 0.7 broadcast_in_dim.7
  1.5 0.1 le.19
  1.6 0.1 compare_and_fusion.1
  1.7 0.1 ge.16
  1.8 0.1 broadcast_compare_fusion
  1.9 0.3 compare_and_fusion
  2.3 1.1 add_convert_fusion.mask_ref
  3.4 2.4 copy.12
  5.8 314.3 %block.1 = (bf16[6,128,768]{2,1,0:T(8,128)(2,1)}, bf16[6,8,8,8,768]{4,3,2,1,0:T(8,128)(2,1)}, bf16[6,8,8,8,768]{4,3,2,1,0:T(8,128)(2,1)}) custom-call(bf16[6,128,768]{2,1,0:T(8,128)(2,1)} %bitcast.14, bf16[8,48,8,768]{3,2,1,0:T(8,128)(2,1)} %bitcast.12, bf16[8,48,8,768]{3,2,1,0:T(8,128)(2,1)} %bitcast.13, bf16[6,128,640]{2,1,0:T(8,128)(2,1)} %add_convert_fusion.mask_ref, ...), custom_call_target="tpu_custom_call" | custom-call | tf_op jit(solution)/shard_map/block/pallas_call | solution.py:445
  320.1 2.4 copy.13
  (5 shorter events, 0.0 us)
